TPU v7x, 32 devices: a whole 2x2x4 slice. The times are simulated.
32 devices in a mesh: rows: 4 (over y, x), seq: 8 (over z, core).
Axes of the slice: x: 2, y: 2, z: 4, core: 2. Of those that a mesh axis runs over, the one named last changes fastest.
Arguments:
- inputs: bfloat16 [8, 2048, 768], P('rows', 'seq'), may hold values from -6 to 6
- doc_lengths: int32 [8, 2], P('rows'), may hold values from 0 to 2048, as said below
- w_query: bfloat16 [768, 768], replicated, may hold values from -0.0546875 to 0.0546875
- w_key: bfloat16 [768, 768], replicated, may hold values from -0.21875 to 0.21875
- w_value: bfloat16 [768, 768], replicated, may hold values from -0.21875 to 0.21875
- w_out: bfloat16 [768, 768], replicated, may hold values from -1.25 to 1.25
- w_in: bfloat16 [768, 3072], replicated, may hold values from -0.21875 to 0.21875
- w_ffout: bfloat16 [3072, 768], replicated, may hold values from -0.109375 to 0.109375
- rel_table: float32 [32, 12], replicated, may hold values from -4 to 4
- gain_attn: float32 [768], replicated, may hold values from 0.25 to 1.75
- gain_ffn: float32 [768], replicated, may hold values from 0.25 to 1.75
- phm_rule: float32 [4, 4, 4], replicated, may hold values from -4 to 4
- down_left: float32 [4, 192], replicated, may hold values from -0.109375 to 0.109375
- down_right: float32 [4, 12], replicated, may hold values from -4 to 4
- up_left: float32 [4, 12], replicated, may hold values from -4 to 4
- up_right: float32 [4, 192], replicated, may hold values from -0.4375 to 0.4375
- down_bias: float32 [48], replicated, may hold values from -3 to 3
- up_bias: float32 [768], replicated, may hold values from -2 to 2
- cotangent: bfloat16 [8, 2048, 768], P('rows', 'seq'), may hold values from -10 to 10
Outputs:
- output: bfloat16 [8, 2048, 768], P('rows', 'seq')
- input_grad: bfloat16 [8, 2048, 768], P('rows', 'seq')
- rule_grad: float32 [4, 4, 4], replicated
- down_left_grad: float32 [4, 192], replicated
- down_right_grad: float32 [4, 12], replicated
- up_left_grad: float32 [4, 12], replicated
- up_right_grad: float32 [4, 192], replicated
- down_bias_grad: float32 [48], replicated
- up_bias_grad: float32 [768], replicated
Inputs may be any that keep to these rules, and one draw needn't show every extreme that they name: `doc_lengths`: each row's nonzero lengths come first, are at least 1024 and add up to 2048; the rest are 0. In each aligned block of 2 rows that one index of rows holds, exactly one row is a single document; every other row holds two documents or more.
All inputs are finite; a program needn't handle non-finite values.
Results may differ from a plain program's by a relative error of at most 0.035.
Values may be sent and summed in bfloat16 or wider, within the bound.
A program may use at most 256 MiB of HBM per device.

v0:
```python
import math

import jax
import jax.numpy as jnp
from jax import lax
from jax.sharding import PartitionSpec as P

epsilon = 1e-06
highest = lax.Precision.HIGHEST
bucket_edges = (12, 16, 23, 32, 46, 64, 91)


def smooth_gelu(values):
    return (
        0.5
        * values
        * (1.0 + jnp.tanh(0.7978845608028654 * (values + 0.044715 * values * values * values)))
    )


def rms_norm(values, gain):
    return values * lax.rsqrt(jnp.mean(values * values, axis=-1, keepdims=True) + epsilon) * gain


def bucket_of(offset):
    magnitude = jnp.abs(offset)
    larger = jnp.full(offset.shape, 8, jnp.int32)
    for edge in bucket_edges:
        larger = larger + (magnitude >= edge).astype(jnp.int32)
    inside = jnp.where(magnitude < 8, magnitude, larger)
    return inside + jnp.where(offset > 0, 16, 0).astype(jnp.int32)


def segment_ids(lengths, token_positions):
    doc_ends = jnp.cumsum(lengths, axis=-1, dtype=jnp.int32)
    return jnp.sum(
        (token_positions[..., :, None] >= doc_ends[..., None, :]).astype(jnp.int32),
        axis=-1,
        dtype=jnp.int32,
    )


def kron_sum(rule_part, left_part, right_part):
    blocks = jnp.einsum("iab,ip,iq->apbq", rule_part, left_part, right_part, precision=highest)
    return blocks.reshape(
        rule_part.shape[1] * left_part.shape[1], rule_part.shape[2] * right_part.shape[1]
    )


def pair_bias(query_pos, key_pos, rel_table):
    buckets = bucket_of(key_pos[None, :] - query_pos[:, None])
    onehot = (buckets[:, :, None] == jnp.arange(rel_table.shape[0], dtype=jnp.int32)).astype(
        jnp.bfloat16
    )
    table_high = rel_table.astype(jnp.bfloat16)
    table_rest = (rel_table - table_high.astype(jnp.float32)).astype(jnp.bfloat16)
    high_part = jnp.einsum("qkb,bh->qhk", onehot, table_high, preferred_element_type=jnp.float32)
    rest_part = jnp.einsum("qkb,bh->qhk", onehot, table_rest, preferred_element_type=jnp.float32)
    return high_part + rest_part


def over_blocks(carried, pieces, blockwise):
    total_len = pieces[0].shape[1]
    block_len = math.gcd(total_len, 512)

    def one_step(block_index, inner_state):
        begin_row = block_index * block_len
        sliced = tuple(
            (lax.dynamic_slice_in_dim(member, begin_row, block_len, 1) for member in pieces)
        )
        return blockwise(inner_state, sliced, begin_row)

    return lax.fori_loop(0, total_len // block_len, one_step, carried)


def local(
    inputs,
    doc_lengths,
    w_query,
    w_key,
    w_value,
    w_out,
    w_in,
    w_ffout,
    rel_table,
    gain_attn,
    gain_ffn,
    phm_rule,
    down_left,
    down_right,
    up_left,
    up_right,
    down_bias,
    up_bias,
    cotangent,
):
    row_count, length, model_width = inputs.shape
    head_count = rel_table.shape[1]
    head_dim = model_width // head_count
    seq_place = lax.axis_index("seq")
    token_count = row_count * length
    local_pos = seq_place * length + jnp.arange(length, dtype=jnp.int32)
    local_seg = segment_ids(doc_lengths, local_pos[None, :])
    bf16 = jnp.bfloat16
    f32 = jnp.float32

    def heads_of(matrix, block_len):
        return matrix.reshape(row_count, block_len, head_count, head_dim)

    def norm_attn(values):
        return rms_norm(values, gain_attn)

    def norm_ffn(values):
        return rms_norm(values, gain_ffn)

    source = inputs.astype(f32).reshape(token_count, model_width)
    normed, norm_attn_back = jax.vjp(norm_attn, source)
    normed_b = normed.astype(bf16)
    queries = (
        jnp.dot(normed_b, w_query, preferred_element_type=f32)
        .astype(bf16)
        .reshape(row_count, length, model_width)
    )
    key_rows = (
        jnp.dot(normed_b, w_key, preferred_element_type=f32)
        .astype(bf16)
        .reshape(row_count, length, model_width)
    )
    value_rows = (
        jnp.dot(normed_b, w_value, preferred_element_type=f32)
        .astype(bf16)
        .reshape(row_count, length, model_width)
    )
    queries_h = heads_of(queries, length)
    keys_h = heads_of(key_rows, length)
    values_h = heads_of(value_rows, length)

    def scores_for(query_h, query_pos, query_seg, key_h, key_pos, key_seg):
        scores = jnp.einsum("rqhd,rkhd->rqhk", query_h, key_h, preferred_element_type=f32)
        scores = scores + pair_bias(query_pos, key_pos, rel_table)[None]
        allowed = (query_seg[:, :, None] == key_seg[:, None, :])[:, :, None, :]
        return (scores, allowed)

    def forward_piece(carried, pieces, first_row):
        weighted, running, mass_sum = carried
        key_part, value_part = pieces
        block_len = key_part.shape[1]
        key_pos = first_row + jnp.arange(block_len, dtype=jnp.int32)
        key_seg = segment_ids(doc_lengths, key_pos[None, :])
        scores, allowed = scores_for(
            queries_h, local_pos, local_seg, heads_of(key_part, block_len), key_pos, key_seg
        )
        scores = jnp.where(allowed, scores, -1e30)
        raised = jnp.maximum(running, jnp.max(scores, axis=-1))
        weights = jnp.where(allowed, jnp.exp(scores - raised[..., None]), 0.0)
        rescale = jnp.exp(running - raised)
        mass_sum = mass_sum * rescale + jnp.sum(weights, axis=-1)
        weighted = weighted * rescale[..., None] + jnp.einsum(
            "rqhk,rkhd->rqhd",
            weights.astype(bf16),
            heads_of(value_part, block_len),
            preferred_element_type=f32,
        )
        return (weighted, raised, mass_sum)

    start_state = (
        jnp.zeros((row_count, length, head_count, head_dim), f32),
        jnp.full((row_count, length, head_count), -1e30, f32),
        jnp.zeros((row_count, length, head_count), f32),
    )
    weighted, running, mass_sum = over_blocks(
        start_state,
        (
            lax.all_gather(key_rows, "seq", axis=1, tiled=True),
            lax.all_gather(value_rows, "seq", axis=1, tiled=True),
        ),
        forward_piece,
    )
    attended = weighted / mass_sum[..., None]
    log_mass = running + jnp.log(mass_sum)
    attended_b = attended.astype(bf16).reshape(token_count, model_width)
    hidden = source + jnp.dot(attended_b, w_out, preferred_element_type=f32)
    normed_ffn, norm_ffn_back = jax.vjp(norm_ffn, hidden)
    inner = jnp.dot(normed_ffn.astype(bf16), w_in, preferred_element_type=f32)
    activated, gelu_back = jax.vjp(smooth_gelu, inner)
    activated_b = activated.astype(bf16)
    ff_out = jnp.dot(activated_b, w_ffout, preferred_element_type=f32).astype(bf16)
    down_full, down_back = jax.vjp(kron_sum, phm_rule, down_left, down_right)
    up_full, up_back = jax.vjp(kron_sum, phm_rule, up_left, up_right)
    down_b = down_full.astype(bf16)
    up_b = up_full.astype(bf16)
    squeezed = jnp.dot(ff_out, down_b, preferred_element_type=f32) + down_bias
    squeezed_act, squeeze_back = jax.vjp(smooth_gelu, squeezed)
    squeezed_act_b = squeezed_act.astype(bf16)
    expanded = jnp.dot(squeezed_act_b, up_b, preferred_element_type=f32) + up_bias
    result = hidden + ff_out.astype(f32) + expanded
    output = result.astype(bf16).reshape(row_count, length, model_width)
    upstream = cotangent.astype(f32).reshape(token_count, model_width)
    up_bias_grad = jnp.sum(upstream, axis=0)
    upstream_b = upstream.astype(bf16)
    up_matrix_grad = jnp.einsum("ta,td->ad", squeezed_act_b, upstream_b, preferred_element_type=f32)
    squeezed_grad = squeeze_back(
        jnp.einsum("td,ad->ta", upstream_b, up_b, preferred_element_type=f32)
    )[0]
    down_bias_grad = jnp.sum(squeezed_grad, axis=0)
    squeezed_low = squeezed_grad.astype(bf16)
    down_matrix_grad = jnp.einsum("td,ta->da", ff_out, squeezed_low, preferred_element_type=f32)
    rule_down, down_left_grad, down_right_grad = down_back(down_matrix_grad)
    rule_up, up_left_grad, up_right_grad = up_back(up_matrix_grad)
    summed = lax.psum(
        (
            rule_down + rule_up,
            down_left_grad,
            down_right_grad,
            up_left_grad,
            up_right_grad,
            down_bias_grad,
            up_bias_grad,
        ),
        ("rows", "seq"),
    )
    ff_grad = upstream + jnp.einsum("ta,da->td", squeezed_low, down_b, preferred_element_type=f32)
    ff_grad_b = ff_grad.astype(bf16)
    inner_grad = gelu_back(jnp.einsum("td,fd->tf", ff_grad_b, w_ffout, preferred_element_type=f32))[
        0
    ]
    inner_grad_b = inner_grad.astype(bf16)
    hidden_grad = (
        upstream
        + norm_ffn_back(jnp.einsum("tf,df->td", inner_grad_b, w_in, preferred_element_type=f32))[0]
    )
    hidden_grad_b = hidden_grad.astype(bf16)
    attended_grad = jnp.einsum(
        "te,de->td", hidden_grad_b, w_out, preferred_element_type=f32
    ).astype(bf16)
    attended_grad = attended_grad.reshape(row_count, length, model_width)
    attended_grad_h = heads_of(attended_grad, length)
    row_delta = jnp.sum(attended_grad_h.astype(f32) * attended, axis=-1)

    def gradient_terms(
        query_h,
        query_pos,
        query_seg,
        grad_h,
        mass_part,
        delta_part,
        key_h,
        value_h,
        key_pos,
        key_seg,
    ):
        scores, allowed = scores_for(query_h, query_pos, query_seg, key_h, key_pos, key_seg)
        weights = jnp.exp(jnp.where(allowed, scores - mass_part[..., None], -1e30))
        weights_grad = jnp.einsum("rqhd,rkhd->rqhk", grad_h, value_h, preferred_element_type=f32)
        score_grad = (weights * (weights_grad - delta_part[..., None])).astype(bf16)
        return (weights.astype(bf16), score_grad)

    zero_grad = jnp.zeros((row_count, length, head_count, head_dim), f32)

    def query_side(carried, pieces, first_row):
        key_part, value_part = pieces
        block_len = key_part.shape[1]
        key_pos = first_row + jnp.arange(block_len, dtype=jnp.int32)
        key_seg = segment_ids(doc_lengths, key_pos[None, :])
        key_h = heads_of(key_part, block_len)
        weights_b, score_grad = gradient_terms(
            queries_h,
            local_pos,
            local_seg,
            attended_grad_h,
            log_mass,
            row_delta,
            key_h,
            heads_of(value_part, block_len),
            key_pos,
            key_seg,
        )
        return carried + jnp.einsum(
            "rqhk,rkhd->rqhd", score_grad, key_h, preferred_element_type=f32
        )

    query_grad = over_blocks(
        zero_grad,
        (
            lax.all_gather(key_rows, "seq", axis=1, tiled=True),
            lax.all_gather(value_rows, "seq", axis=1, tiled=True),
        ),
        query_side,
    )
    mass_all, delta_all = (
        lax.all_gather(log_mass, "seq", axis=1, tiled=True),
        lax.all_gather(row_delta, "seq", axis=1, tiled=True),
    )

    def key_side(carried, pieces, first_row):
        key_acc, value_acc = carried
        query_part, grad_part = pieces
        block_len = query_part.shape[1]
        query_pos = first_row + jnp.arange(block_len, dtype=jnp.int32)
        query_seg = segment_ids(doc_lengths, query_pos[None, :])
        mass_part = lax.dynamic_slice_in_dim(mass_all, first_row, block_len, 1)
        delta_part = lax.dynamic_slice_in_dim(delta_all, first_row, block_len, 1)
        query_h = heads_of(query_part, block_len)
        grad_h = heads_of(grad_part, block_len)
        weights_b, score_grad = gradient_terms(
            query_h,
            query_pos,
            query_seg,
            grad_h,
            mass_part,
            delta_part,
            keys_h,
            values_h,
            local_pos,
            local_seg,
        )
        key_acc = key_acc + jnp.einsum(
            "rqhk,rqhd->rkhd", score_grad, query_h, preferred_element_type=f32
        )
        value_acc = value_acc + jnp.einsum(
            "rqhk,rqhd->rkhd", weights_b, grad_h, preferred_element_type=f32
        )
        return (key_acc, value_acc)

    key_grad, value_grad = over_blocks(
        (zero_grad, zero_grad),
        (
            lax.all_gather(queries, "seq", axis=1, tiled=True),
            lax.all_gather(attended_grad, "seq", axis=1, tiled=True),
        ),
        key_side,
    )
    query_grad_b = query_grad.astype(bf16).reshape(token_count, model_width)
    key_grad_b = key_grad.astype(bf16).reshape(token_count, model_width)
    value_grad_b = value_grad.astype(bf16).reshape(token_count, model_width)
    normed_grad = jnp.einsum("te,de->td", query_grad_b, w_query, preferred_element_type=f32)
    normed_grad = normed_grad + jnp.einsum(
        "te,de->td", key_grad_b, w_key, preferred_element_type=f32
    )
    normed_grad = normed_grad + jnp.einsum(
        "te,de->td", value_grad_b, w_value, preferred_element_type=f32
    )
    input_grad = hidden_grad + norm_attn_back(normed_grad)[0]
    input_grad = input_grad.astype(bf16).reshape(row_count, length, model_width)
    return (
        output,
        input_grad,
        summed[0],
        summed[1],
        summed[2],
        summed[3],
        summed[4],
        summed[5],
        summed[6],
    )


def solution(mesh):
    return jax.shard_map(
        local,
        mesh=mesh,
        in_specs=(
            P("rows", "seq", None),
            P("rows", None),
            P(),
            P(),
            P(),
            P(),
            P(),
            P(),
            P(),
            P(),
            P(),
            P(),
            P(),
            P(),
            P(),
            P(),
            P(),
            P(),
            P("rows", "seq", None),
        ),
        out_specs=(
            P("rows", "seq", None),
            P("rows", "seq", None),
            P(),
            P(),
            P(),
            P(),
            P(),
            P(),
            P(),
        ),
        check_vma=False,
    )
```

profile of v0, /device:TPU:0, one launch (start us, length us, event | category | flops | bytes accessed | tf_op | source)
XLA Modules:
  0.0 886.2 jit_solution(2115039749613443053)
XLA Ops:
  42.9 39.9 %all-gather.5.cloned.1.call-done = bf16[2,2048,768]{1,2,0:T(8,128)(2,1)} async-done(((bf16[2,256,768]{1,2,0:T(8,128)(2,1)}), bf16[2,2048,768]{1,2,0:T(8,128)(2,1)}) %all-gather.5.cloned.1.call-update) | async-done | bytes 6291472 | tf_op jit(solution)/shard_map/all_gather | solution.py:174
  82.8 65.0 %all-gather.7.cloned.1.call-done = bf16[2,2048,768]{1,2,0:T(8,128)(2,1)} async-done(((bf16[2,256,768]{1,2,0:T(8,128)(2,1)}), bf16[2,2048,768]{1,2,0:T(8,128)(2,1)}) %all-gather.7.cloned.1.call-update) | async-done | bytes 6291472 | tf_op jit(solution)/shard_map/all_gather | solution.py:175
  147.8 201.9 %while.54 = (s32[]{:T(128)}, f32[2,256,12,64]{1,3,2,0:T(8,128)}, f32[2,256,12]{1,2,0:T(8,128)S(1)}, f32[2,256,12]{1,2,0:T(8,128)S(1)}, s32[2,256]{1,0:T(2,128)S(...) while((s32[]{:T(128)}, f32[2,256,12,64]{1,3,2,0:T(8,128)}, ...), condition=%wide.region_7.8_spmd.clone, body=%wide.region_3.7_spmd.clone.sunk | while | flops 1062638464 | bytes 161109360 | solution.py:73
  151.2 6.7 bitcast_add_fusion.19
  157.9 9.3 %copy.172 = f32[256,12,512]{0,2,1:T(8,128)} copy(f32[256,12,512]{2,1,0:T(8,128)} %bitcast_add_fusion.19) | data formatting | bytes 12582912 | tf_op jit(solution)/shard_map/while/body/eval_jaxpr/add | solution.py:59
  171.2 7.2 fusion.288
  178.4 8.8 fusion.289
  187.3 7.3 bitcast_add_fusion.20
  205.6 9.2 %copy.172 = f32[256,12,512]{0,2,1:T(8,128)} copy(f32[256,12,512]{2,1,0:T(8,128)} %bitcast_add_fusion.19) | data formatting | bytes 12582912 | tf_op jit(solution)/shard_map/while/body/eval_jaxpr/add | solution.py:59
  218.6 7.1 fusion.288
  225.7 8.8 fusion.289
  234.5 7.1 bitcast_add_fusion.20
  246.0 6.6 bitcast_add_fusion.19
  252.6 9.2 %copy.172 = f32[256,12,512]{0,2,1:T(8,128)} copy(f32[256,12,512]{2,1,0:T(8,128)} %bitcast_add_fusion.19) | data formatting | bytes 12582912 | tf_op jit(solution)/shard_map/while/body/eval_jaxpr/add | solution.py:59
  265.6 7.1 fusion.288
  272.8 8.8 fusion.289
  281.6 7.1 bitcast_add_fusion.20
  293.0 6.6 bitcast_add_fusion.19
  299.7 9.2 %copy.172 = f32[256,12,512]{0,2,1:T(8,128)} copy(f32[256,12,512]{2,1,0:T(8,128)} %bitcast_add_fusion.19) | data formatting | bytes 12582912 | tf_op jit(solution)/shard_map/while/body/eval_jaxpr/add | solution.py:59
  312.7 7.1 fusion.288
  319.8 8.8 fusion.289
  328.6 7.1 bitcast_add_fusion.20
  369.1 15.4 %multiply_reduce_fusion.1 = (f32[512]{0:T(512)}, f32[512,768]{1,0:T(8,128)}) fusion(f32[512,768]{1,0:T(8,128)S(1)} %get-tuple-element.1237, f32[768]{0:T(1024)} %param.35, bf16[768,3072]{1,0:T(8,128)(2,1)} %param.31, f32[512,3072]{1,0:T(8,128)} %copy-done.19, bf16[512,768]{1,0:T(8,128)(2,1)} %fusion.111, bf16[3072,768]{1,0:T(8,128)(2,1)} %param.32), kind=kOutput, calls=%fused_computation.165 | convolution fusion | flops 4870766080 | bytes 19665920 | tf_op jit(solution)/shard_map/tf,df->td/dot_general | solution.py:230
  396.9 172.0 %while.55 = (s32[]{:T(128)}, f32[2,256,12,64]{1,3,2,0:T(8,128)}, bf16[2,2048,768]{1,2,0:T(8,128)(2,1)}, s32[2,256]{1,0:T(2,128)S(1)}, s32[2,1,2]{2,0,1:T(2,128)}...) while((s32[]{:T(128)}, f32[2,256,12,64]{1,3,2,0:T(8,128)}, ...), condition=%wide.region_13.14_spmd.clone, body=%wide.region_11.13_spmd.clone.sunk | while | flops 1442847616 | bytes 83957008 | solution.py:73
  407.1 9.2 %copy.173 = f32[256,12,512]{0,2,1:T(8,128)} copy(f32[256,12,512]{2,1,0:T(8,128)} %bitcast_add_fusion.21) | data formatting | bytes 12582912 | tf_op jit(solution)/shard_map/while/body/eval_jaxpr/add | solution.py:59
  427.0 12.9 %bitcast_add_fusion.22 = f32[2,256,12,64]{1,3,2,0:T(8,128)} fusion(f32[2,256,12,64]{1,3,2,0:T(8,128)} %get-tuple-element.1625, bf16[2,512,12,64]{1,3,2,0:T(8,128)(2,1)S(1)} %bitcast.397, f32[2,12,512,256]{3,2,1,0:T(8,128)} %fusion.299, f32[2,256,12]{1,2,0:T(8,128)S(1)} %get-tuple-element.1652, f32[2,256,12]{1,2,0:T(8,128)S(1)} %get-tuple-element.1649, ...), kind=kOutput, calls=%fused_computation.62.clone.1 | convolution fusion | flops 824967168 | bytes 26263552 | tf_op jit(solution)/shard_map/while/body/eval_jaxpr/rqhk,rkhd->rqhd/dot_general | solution.py:278
  449.7 9.2 %copy.173 = f32[256,12,512]{0,2,1:T(8,128)} copy(f32[256,12,512]{2,1,0:T(8,128)} %bitcast_add_fusion.21) | data formatting | bytes 12582912 | tf_op jit(solution)/shard_map/while/body/eval_jaxpr/add | solution.py:59
  469.7 13.3 %bitcast_add_fusion.22 = f32[2,256,12,64]{1,3,2,0:T(8,128)} fusion(f32[2,256,12,64]{1,3,2,0:T(8,128)} %get-tuple-element.1625, bf16[2,512,12,64]{1,3,2,0:T(8,128)(2,1)S(1)} %bitcast.397, f32[2,12,512,256]{3,2,1,0:T(8,128)} %fusion.299, f32[2,256,12]{1,2,0:T(8,128)S(1)} %get-tuple-element.1652, f32[2,256,12]{1,2,0:T(8,128)S(1)} %get-tuple-element.1649, ...), kind=kOutput, calls=%fused_computation.62.clone.1 | convolution fusion | flops 824967168 | bytes 26263552 | tf_op jit(solution)/shard_map/while/body/eval_jaxpr/rqhk,rkhd->rqhd/dot_general | solution.py:278
  492.7 9.2 %copy.173 = f32[256,12,512]{0,2,1:T(8,128)} copy(f32[256,12,512]{2,1,0:T(8,128)} %bitcast_add_fusion.21) | data formatting | bytes 12582912 | tf_op jit(solution)/shard_map/while/body/eval_jaxpr/add | solution.py:59
  512.6 13.3 %bitcast_add_fusion.22 = f32[2,256,12,64]{1,3,2,0:T(8,128)} fusion(f32[2,256,12,64]{1,3,2,0:T(8,128)} %get-tuple-element.1625, bf16[2,512,12,64]{1,3,2,0:T(8,128)(2,1)S(1)} %bitcast.397, f32[2,12,512,256]{3,2,1,0:T(8,128)} %fusion.299, f32[2,256,12]{1,2,0:T(8,128)S(1)} %get-tuple-element.1652, f32[2,256,12]{1,2,0:T(8,128)S(1)} %get-tuple-element.1649, ...), kind=kOutput, calls=%fused_computation.62.clone.1 | convolution fusion | flops 824967168 | bytes 26263552 | tf_op jit(solution)/shard_map/while/body/eval_jaxpr/rqhk,rkhd->rqhd/dot_general | solution.py:278
  535.6 9.2 %copy.173 = f32[256,12,512]{0,2,1:T(8,128)} copy(f32[256,12,512]{2,1,0:T(8,128)} %bitcast_add_fusion.21) | data formatting | bytes 12582912 | tf_op jit(solution)/shard_map/while/body/eval_jaxpr/add | solution.py:59
  555.4 13.3 %bitcast_add_fusion.22 = f32[2,256,12,64]{1,3,2,0:T(8,128)} fusion(f32[2,256,12,64]{1,3,2,0:T(8,128)} %get-tuple-element.1625, bf16[2,512,12,64]{1,3,2,0:T(8,128)(2,1)S(1)} %bitcast.397, f32[2,12,512,256]{3,2,1,0:T(8,128)} %fusion.299, f32[2,256,12]{1,2,0:T(8,128)S(1)} %get-tuple-element.1652, f32[2,256,12]{1,2,0:T(8,128)S(1)} %get-tuple-element.1649, ...), kind=kOutput, calls=%fused_computation.62.clone.1 | convolution fusion | flops 824967168 | bytes 26263552 | tf_op jit(solution)/shard_map/while/body/eval_jaxpr/rqhk,rkhd->rqhd/dot_general | solution.py:278
  581.9 39.6 %all-reduce = (f32[4,4,4]{2,1,0:T(4,128)}, f32[4,192]{1,0:T(4,128)}, f32[4,12]{1,0:T(4,128)}, f32[4,12]{1,0:T(4,128)}, f32[4,192]{1,0:T(4,128)}, /*index=5*/f32[48]{0:T(128)}, f32[768]{0:T(1024)}) all-reduce(f32[4,4,4]{2,1,0:T(4,128)S(1)} %add.726, ...), channel_id=1, replica_groups=mesh['rows'=4,'seq'=8] {'rows','seq'}, use_global_device_ids=true, to_apply=%region_18.19 | all-reduce | flops 2512 | bytes 20096 | tf_op jit(solution)/shard_map/psum | solution.py:210
  621.5 14.3 %all_gather.25 = f32[2,2048,12]{1,0,2:T(2,128)} all-gather(f32[2,256,12]{1,0,2:T(2,128)} %copy-done.41), channel_id=1, replica_groups=mesh['rows'=4,'seq'=8] {'seq'}, dimensions={1}, use_global_device_ids=true | all-gather | bytes 221184 | tf_op jit(solution)/shard_map/all_gather | solution.py:292
  635.8 15.3 %all_gather.23 = f32[2,2048,12]{1,2,0:T(8,128)} all-gather(f32[2,256,12]{1,2,0:T(8,128)S(1)} %get-tuple-element.1681), channel_id=1, replica_groups=mesh['rows'=4,'seq'=8] {'seq'}, dimensions={1}, use_global_device_ids=true | all-gather | bytes 221184 | tf_op jit(solution)/shard_map/all_gather | solution.py:291
  655.3 215.7 %while.56 = (s32[]{:T(128)}, f32[2,256,12,64]{1,3,2,0:T(8,128)}, f32[2,256,12,64]{1,3,2,0:T(8,128)}, bf16[2,2048,768]{1,2,0:T(8,128)(2,1)}, s32[2,1,2]{2,0,1:T(2...) while((s32[]{:T(128)}, f32[2,256,12,64]{1,3,2,0:T(8,128)}, ...), condition=%wide.region_16.17_spmd.clone, body=%wide.region_14.16_spmd.clone.sunk | while | flops 1858870144 | bytes 114496824 | solution.py:73
  670.5 6.6 bitcast_add_fusion.23
  685.2 9.1 %bitcast_add_fusion.25 = f32[2,256,12,64]{1,3,2,0:T(8,128)} fusion(f32[2,256,12,64]{1,3,2,0:T(8,128)} %get-tuple-element.1573, bf16[2,512,12,64]{1,3,2,0:T(8,128)(2,1)S(1)} %bitcast.392, f32[2,12,512,256]{3,2,1,0:T(8,128)} %fusion.313, f32[2,512,12]{1,2,0:T(8,128)S(1)} %constant_dynamic-slice_fusion.17, f32[512,12,256]{2,0,1:T(8,128)} %copy.175, ...), kind=kOutput, calls=%fused_computation.104.clone.1 | convolution fusion | flops 416022528 | bytes 23904256 | tf_op jit(solution)/shard_map/while/body/eval_jaxpr/rqhk,rqhd->rkhd/dot_general | solution.py:320
  695.1 13.4 %bitcast_add_fusion.24 = f32[2,256,12,64]{1,3,2,0:T(8,128)} fusion(f32[2,256,12,64]{1,3,2,0:T(8,128)} %get-tuple-element.1572, bf16[2,512,12,64]{1,3,2,0:T(8,128)(2,1)} %bitcast.395, f32[2,12,512,256]{3,2,1,0:T(8,128)} %fusion.313, f32[2,512,12]{1,2,0:T(8,128)S(1)} %copy.174, f32[2,512,12]{1,2,0:T(8,128)S(1)} %constant_dynamic-slice_fusion.17, ...), kind=kOutput, calls=%fused_computation.105.clone.1 | convolution fusion | flops 824967168 | bytes 26312704 | tf_op jit(solution)/shard_map/while/body/eval_jaxpr/rqhk,rqhd->rkhd/dot_general | solution.py:317
  723.5 6.6 bitcast_add_fusion.23
  738.2 9.7 %bitcast_add_fusion.25 = f32[2,256,12,64]{1,3,2,0:T(8,128)} fusion(f32[2,256,12,64]{1,3,2,0:T(8,128)} %get-tuple-element.1573, bf16[2,512,12,64]{1,3,2,0:T(8,128)(2,1)S(1)} %bitcast.392, f32[2,12,512,256]{3,2,1,0:T(8,128)} %fusion.313, f32[2,512,12]{1,2,0:T(8,128)S(1)} %constant_dynamic-slice_fusion.17, f32[512,12,256]{2,0,1:T(8,128)} %copy.175, ...), kind=kOutput, calls=%fused_computation.104.clone.1 | convolution fusion | flops 416022528 | bytes 23904256 | tf_op jit(solution)/shard_map/while/body/eval_jaxpr/rqhk,rqhd->rkhd/dot_general | solution.py:320
  748.8 13.9 %bitcast_add_fusion.24 = f32[2,256,12,64]{1,3,2,0:T(8,128)} fusion(f32[2,256,12,64]{1,3,2,0:T(8,128)} %get-tuple-element.1572, bf16[2,512,12,64]{1,3,2,0:T(8,128)(2,1)} %bitcast.395, f32[2,12,512,256]{3,2,1,0:T(8,128)} %fusion.313, f32[2,512,12]{1,2,0:T(8,128)S(1)} %copy.174, f32[2,512,12]{1,2,0:T(8,128)S(1)} %constant_dynamic-slice_fusion.17, ...), kind=kOutput, calls=%fused_computation.105.clone.1 | convolution fusion | flops 824967168 | bytes 26312704 | tf_op jit(solution)/shard_map/while/body/eval_jaxpr/rqhk,rqhd->rkhd/dot_general | solution.py:317
  777.6 6.6 bitcast_add_fusion.23
  792.3 9.7 %bitcast_add_fusion.25 = f32[2,256,12,64]{1,3,2,0:T(8,128)} fusion(f32[2,256,12,64]{1,3,2,0:T(8,128)} %get-tuple-element.1573, bf16[2,512,12,64]{1,3,2,0:T(8,128)(2,1)S(1)} %bitcast.392, f32[2,12,512,256]{3,2,1,0:T(8,128)} %fusion.313, f32[2,512,12]{1,2,0:T(8,128)S(1)} %constant_dynamic-slice_fusion.17, f32[512,12,256]{2,0,1:T(8,128)} %copy.175, ...), kind=kOutput, calls=%fused_computation.104.clone.1 | convolution fusion | flops 416022528 | bytes 23904256 | tf_op jit(solution)/shard_map/while/body/eval_jaxpr/rqhk,rqhd->rkhd/dot_general | solution.py:320
  802.8 13.9 %bitcast_add_fusion.24 = f32[2,256,12,64]{1,3,2,0:T(8,128)} fusion(f32[2,256,12,64]{1,3,2,0:T(8,128)} %get-tuple-element.1572, bf16[2,512,12,64]{1,3,2,0:T(8,128)(2,1)} %bitcast.395, f32[2,12,512,256]{3,2,1,0:T(8,128)} %fusion.313, f32[2,512,12]{1,2,0:T(8,128)S(1)} %copy.174, f32[2,512,12]{1,2,0:T(8,128)S(1)} %constant_dynamic-slice_fusion.17, ...), kind=kOutput, calls=%fused_computation.105.clone.1 | convolution fusion | flops 824967168 | bytes 26312704 | tf_op jit(solution)/shard_map/while/body/eval_jaxpr/rqhk,rqhd->rkhd/dot_general | solution.py:317
  831.6 6.6 bitcast_add_fusion.23
  846.4 9.7 %bitcast_add_fusion.25 = f32[2,256,12,64]{1,3,2,0:T(8,128)} fusion(f32[2,256,12,64]{1,3,2,0:T(8,128)} %get-tuple-element.1573, bf16[2,512,12,64]{1,3,2,0:T(8,128)(2,1)S(1)} %bitcast.392, f32[2,12,512,256]{3,2,1,0:T(8,128)} %fusion.313, f32[2,512,12]{1,2,0:T(8,128)S(1)} %constant_dynamic-slice_fusion.17, f32[512,12,256]{2,0,1:T(8,128)} %copy.175, ...), kind=kOutput, calls=%fused_computation.104.clone.1 | convolution fusion | flops 416022528 | bytes 23904256 | tf_op jit(solution)/shard_map/while/body/eval_jaxpr/rqhk,rqhd->rkhd/dot_general | solution.py:320
  856.9 13.9 %bitcast_add_fusion.24 = f32[2,256,12,64]{1,3,2,0:T(8,128)} fusion(f32[2,256,12,64]{1,3,2,0:T(8,128)} %get-tuple-element.1572, bf16[2,512,12,64]{1,3,2,0:T(8,128)(2,1)} %bitcast.395, f32[2,12,512,256]{3,2,1,0:T(8,128)} %fusion.313, f32[2,512,12]{1,2,0:T(8,128)S(1)} %copy.174, f32[2,512,12]{1,2,0:T(8,128)S(1)} %constant_dynamic-slice_fusion.17, ...), kind=kOutput, calls=%fused_computation.105.clone.1 | convolution fusion | flops 824967168 | bytes 26312704 | tf_op jit(solution)/shard_map/while/body/eval_jaxpr/rqhk,rqhd->rkhd/dot_general | solution.py:317
  (416 shorter events, 308.7 us)
Async XLA Ops:
  7.2 347.1 %copy-start = (bf16[768,768]{1,0:T(8,128)(2,1)S(1)}, bf16[768,768]{1,0:T(8,128)(2,1)}, u32[]{:S(2)}) copy-start(bf16[768,768]{1,0:T(8,128)(2,1)} %param.30) | copy-start | bytes 3538948
  7.2 75.6 %all-gather.5.cloned.1.call-start = ((), (), s32[]{:S(2)}) async-start(), calls=%async_computation | async-start | bytes 7077888 | tf_op jit(solution)/shard_map/all_gather | solution.py:174
  14.8 133.0 %all-gather.7.cloned.1.call-start = ((), (), s32[]{:S(2)}) async-start(), calls=%async_computation.1 | async-start | bytes 7077888 | tf_op jit(solution)/shard_map/all_gather | solution.py:175
  18.1 637.2 %all-gather.9.cloned.1.call-start = ((), (), s32[]{:S(2)}) async-start(), calls=%async_computation.2 | async-start | bytes 7077888 | tf_op jit(solution)/shard_map/all_gather | solution.py:328
  21.7 633.6 %all-gather.11.cloned.1.call-start = ((), (), s32[]{:S(2)}) async-start(), calls=%async_computation.3 | async-start | bytes 7077888 | tf_op jit(solution)/shard_map/all_gather | solution.py:329
  24.6 8.7 copy-start.30
  24.6 8.7 copy-start.57
  24.6 8.9 copy-start.52
  24.6 8.9 copy-start.59
  24.6 10.4 %copy-start.54 = (f32[4,12]{1,0:T(4,128)S(1)}, f32[4,12]{1,0:T(4,128)}, u32[]{:S(2)}) copy-start(f32[4,12]{1,0:T(4,128)} %param.39) | copy-start | bytes 580
  24.6 10.4 %copy-start.60 = (f32[4,192]{1,0:T(4,128)S(1)}, f32[4,192]{1,0:T(4,128)}, u32[]{:S(2)}) copy-start(f32[4,192]{1,0:T(4,128)} %param.40) | copy-start | bytes 9220
  25.8 10.7 %copy-start.28 = (bf16[512,768]{1,0:T(8,128)(2,1)S(1)}, bf16[512,768]{1,0:T(8,128)(2,1)}, u32[]{:S(2)}) copy-start(bf16[512,768]{1,0:T(8,128)(2,1)} %bitcast_convert_fusion) | copy-start | bytes 2359300
  33.5 7.7 copy-start.44
  178.4 8.9 %slice-start = ((s8[6291456]{0:T(1024)(128)(4,1)}), s8[4194304]{0:T(1024)(128)(4,1)S(1)}, s32[]{:S(2)}) async-start(s8[6291456]{0:T(1024)(128)(4,1)} %bitcast.390), calls=%async_computation.4 | async-start | bytes 8388608 | tf_op jit(solution)/shard_map/while
  178.4 8.9 %slice-start.1 = ((s8[6291456]{0:T(1024)(128)(4,1)}), s8[2097152]{0:T(1024)(128)(4,1)S(1)}, s32[]{:S(2)}) async-start(s8[6291456]{0:T(1024)(128)(4,1)} %bitcast.390), calls=%async_computation.5 | async-start | bytes 4194304 | tf_op jit(solution)/shard_map/while
  178.4 8.9 copy-start.6
  225.7 8.8 slice-start
  225.7 8.8 slice-start.1
  225.7 8.8 copy-start.6
  272.7 8.8 slice-start
  272.7 8.8 slice-start.1
  272.7 8.8 copy-start.6
  319.8 8.8 slice-start
  319.8 8.8 slice-start.1
  319.8 8.8 copy-start.6
  355.3 30.0 %copy-start.11 = (f32[512,768]{1,0:T(8,128)}, f32[512,768]{1,0:T(8,128)S(1)}, u32[]{:S(2)}) copy-start(f32[512,768]{1,0:T(8,128)S(1)} %get-tuple-element.1237) | copy-start | bytes 4718596
  359.7 6.5 copy-start.14
  359.7 6.5 copy-start.40
  419.7 7.2 copy-start.10
  462.4 7.2 copy-start.10
  505.3 7.2 copy-start.10
  548.2 7.2 copy-start.10
  570.3 7.9 copy-start.26
  571.3 7.3 copy-start.61
  571.3 8.3 copy-start.55
  571.3 9.3 %copy-start.45 = (f32[4,4,4]{0,2,1:T(4,128)S(1)}, f32[4,4,4]{0,2,1:T(4,128)}, u32[]{:S(2)}) copy-start(f32[4,4,4]{0,2,1:T(4,128)} %copy-done.44) | copy-start | bytes 772
  571.4 9.3 %copy-start.53 = (f32[4,12]{1,0:T(4,128)S(1)}, f32[4,12]{1,0:T(4,128)}, u32[]{:S(2)}) copy-start(f32[4,12]{1,0:T(4,128)} %param.38) | copy-start | bytes 580
  572.9 8.4 copy-start.58
  572.9 78.2 %copy-start.12 = (f32[512,768]{1,0:T(8,128)S(1)}, f32[512,768]{1,0:T(8,128)}, u32[]{:S(2)}) copy-start(f32[512,768]{1,0:T(8,128)} %copy-done.11) | copy-start | bytes 4718596
  572.9 78.2 %copy-start.18 = (bf16[512,768]{1,0:T(8,128)(2,1)S(1)}, bf16[512,768]{1,0:T(8,128)(2,1)}, u32[]{:S(2)}) copy-start(bf16[512,768]{1,0:T(8,128)(2,1)} %copy-done.17) | copy-start | bytes 2359300
  572.9 78.2 %copy-start.39 = (f32[512,48]{0,1:T(8,128)S(1)}, f32[512,48]{0,1:T(8,128)}, u32[]{:S(2)}) copy-start(f32[512,48]{0,1:T(8,128)} %copy-done.38) | copy-start | bytes 294916
  621.5 31.8 %copy-start.35 = (bf16[96,8,2,256]{3,1,2,0:T(8,128)(2,1)S(1)}, bf16[96,8,2,256]{3,1,2,0:T(8,128)(2,1)}, u32[]{:S(2)}) copy-start(bf16[96,8,2,256]{3,1,2,0:T(8,128)(2,1)} %copy.147) | copy-start | bytes 2359300
  621.5 31.8 %copy-start.64 = (bf16[768,768]{1,0:T(8,128)(2,1)S(1)}, bf16[768,768]{1,0:T(8,128)(2,1)}, u32[]{:S(2)}) copy-start(bf16[768,768]{1,0:T(8,128)(2,1)} %param.27) | copy-start | bytes 3538948
  685.2 9.9 %copy-start.9 = (bf16[2,256,12,64]{1,3,2,0:T(8,128)(2,1)S(1)}, bf16[2,256,12,64]{1,3,2,0:T(8,128)(2,1)}, u32[]{:S(2)}) copy-start(bf16[2,256,12,64]{1,3,2,0:T(8,128)(2,1)} %get-tuple-element.1600) | copy-start | bytes 2359300 | tf_op jit(solution)/shard_map/while
  738.2 10.5 %copy-start.9 = (bf16[2,256,12,64]{1,3,2,0:T(8,128)(2,1)S(1)}, bf16[2,256,12,64]{1,3,2,0:T(8,128)(2,1)}, u32[]{:S(2)}) copy-start(bf16[2,256,12,64]{1,3,2,0:T(8,128)(2,1)} %get-tuple-element.1600) | copy-start | bytes 2359300 | tf_op jit(solution)/shard_map/while
  764.7 6.5 copy-start.3
  792.3 10.5 %copy-start.9 = (bf16[2,256,12,64]{1,3,2,0:T(8,128)(2,1)S(1)}, bf16[2,256,12,64]{1,3,2,0:T(8,128)(2,1)}, u32[]{:S(2)}) copy-start(bf16[2,256,12,64]{1,3,2,0:T(8,128)(2,1)} %get-tuple-element.1600) | copy-start | bytes 2359300 | tf_op jit(solution)/shard_map/while
  846.4 10.5 %copy-start.9 = (bf16[2,256,12,64]{1,3,2,0:T(8,128)(2,1)S(1)}, bf16[2,256,12,64]{1,3,2,0:T(8,128)(2,1)}, u32[]{:S(2)}) copy-start(bf16[2,256,12,64]{1,3,2,0:T(8,128)(2,1)} %get-tuple-element.1600) | copy-start | bytes 2359300 | tf_op jit(solution)/shard_map/while
  (50 other events, 147.7 us)
Sparse Core Ops, SparseCore 0:
  14.9 67.8 all-gather.4
  84.4 63.3 all-gather.6
  149.4 63.3 all-gather.8
  397.0 63.4 all-gather.10
where the time goes:
time: 896 us; the launch traced here: 886 us
  matrix products  427 us (48%)
  local copies, waits for them, and re-layouts  182 us (20%)
  waiting for transfers between devices  105 us (12%)
  other arithmetic  72.9 us (8%)
  blocking collectives  69.2 us (8%)
  between operations  15.1 us (2%)
  loops' own time  14.8 us (2%)
    add x12, local copies, waits for them, and re-layouts, pair_bias(): return high_part + rest_part  99 us
    dot_general x12, matrix products, pair_bias(): jnp.einsum('qkb,bh->qhk', onehot, table_high, preferred_element_type=jnp....  79.6 us
    dot_general x12, matrix products, scores_for(): jnp.einsum('rqhd,rkhd->rqhk', query_h, key_h, preferred_element_type=f32)  79.5 us
    all_gather x1, waiting for transfers between devices, local(): lax.all_gather(value_rows, 'seq', axis=1, tiled=True)  65 us
    dot_general x4, matrix products, key_side(): jnp.einsum('rqhk,rqhd->rkhd', score_grad, query_h, preferred_element_type...  55 us
    dot_general x4, matrix products, query_side(): jnp.einsum('rqhk,rkhd->rqhd', score_grad, key_h, preferred_element_type=f32)  52.7 us
    dot_general x12, matrix products, pair_bias(): jnp.einsum('qkb,bh->qhk', onehot, table_rest, preferred_element_type=jnp....  43.5 us
    all_gather x1, waiting for transfers between devices, local(): lax.all_gather(key_rows, 'seq', axis=1, tiled=True)  39.9 us
  transfers between devices with their start and end apart: 4, of which 2 were waited for; matrix products, arithmetic and copies ran while one was open for 50% of the time, Pallas kernels for 0%

commit v1 on v0

--- a/solution.py
+++ b/solution.py
@@ -1,8 +1,11 @@
+import functools
 import math
 
 import jax
 import jax.numpy as jnp
 from jax import lax
+from jax.experimental import pallas as pl
+from jax.experimental.pallas import tpu as pltpu
 from jax.sharding import PartitionSpec as P
 
 epsilon = 1e-06
@@ -355,9 +358,950 @@
     )
 
 
+MESH = pl.DeviceIdType.MESH
+LANES = 256
+
+
+def dot_nn(left, right, precision=None):
+    return lax.dot_general(
+        left, right, (((1,), (0,)), ((), ())), precision=precision, preferred_element_type=jnp.float32
+    )
+
+
+def dot_nt(left, right, precision=None):
+    return lax.dot_general(
+        left, right, (((1,), (1,)), ((), ())), precision=precision, preferred_element_type=jnp.float32
+    )
+
+
+def gelu_pair(values):
+    square = values * values
+    tanh = jnp.tanh(0.7978845608028654 * values * (1.0 + 0.044715 * square))
+    half = 0.5 * (1.0 + tanh)
+    slope = half + 0.5 * values * (1.0 - tanh * tanh) * (
+        0.7978845608028654 * (1.0 + 3.0 * 0.044715 * square)
+    )
+    return values * half, slope
+
+
+def inverse_rms(values):
+    return lax.rsqrt(jnp.mean(values * values, axis=-1, keepdims=True) + epsilon)
+
+
+def norm_back(values, gain, grad):
+    inverse = inverse_rms(values)
+    scaled = grad * gain
+    return inverse * scaled - values * (
+        inverse * inverse * inverse * jnp.mean(values * scaled, axis=-1, keepdims=True)
+    )
+
+
+def layer_kernel(
+    rows_size,
+    doc_lengths,
+    rel_table,
+    phm_rule,
+    gain_attn,
+    gain_ffn,
+    down_left,
+    down_right,
+    up_left,
+    up_right,
+    down_bias,
+    up_bias,
+    x_hbm,
+    ct_hbm,
+    w_query_hbm,
+    w_key_hbm,
+    w_value_hbm,
+    w_out_hbm,
+    w_in_hbm,
+    w_ffout_hbm,
+    out_hbm,
+    igrad_hbm,
+    stats_out,
+    w_query,
+    w_key,
+    w_value,
+    w_out,
+    w_in,
+    w_ffout,
+    x_rows,
+    ct_rows,
+    normed,
+    qkv_send,
+    slots_a,
+    slots_b,
+    key_value,
+    wide,
+    bias,
+    att_a,
+    att_b,
+    mass_a,
+    mass_b,
+    o_send_a,
+    o_send_b,
+    att_recv,
+    hidden,
+    act,
+    ff_out,
+    down_b,
+    up_b,
+    hidden_grad,
+    do_a,
+    do_b,
+    dk_acc,
+    dv_acc,
+    dq_acc,
+    stats,
+    stats_rows,
+    stats_core,
+    stats_z,
+    out_stage,
+    load_sem,
+    qkv_send_sem,
+    slot_a_sem,
+    slot_b_sem,
+    o_send_a_sem,
+    o_send_b_sem,
+    att_sem,
+    do_send_sem,
+    do_a_sem,
+    do_b_sem,
+    g_send_a_sem,
+    g_send_b_sem,
+    g_sem,
+    st_rows_send,
+    st_rows_recv,
+    st_core_send,
+    st_core_recv,
+    st_z_send,
+    st_z_recv,
+    st_last_send,
+    st_last_recv,
+    out_sem,
+):
+    f32 = jnp.float32
+    bf16 = jnp.bfloat16
+    highest_p = lax.Precision.HIGHEST
+    row_place = lax.axis_index("rows")
+    place = lax.axis_index("seq")
+    chip = place // 2
+    core = lax.rem(place, 2)
+    half = chip // 2
+    parity = lax.rem(chip, 2)
+
+    gain_attn = gain_attn[...].reshape(1, 768)
+    gain_ffn = gain_ffn[...].reshape(1, 768)
+    down_bias = down_bias[...].reshape(1, 48)
+    up_bias = up_bias[...].reshape(1, 768)
+
+    x_raw = out_stage.at[0]
+    ct_raw = out_stage.at[1]
+    do_send = att_recv
+    g_recv = qkv_send
+
+    loads = [
+        pltpu.make_async_copy(src, dst, load_sem.at[index])
+        for index, (src, dst) in enumerate(
+            (
+                (x_hbm, x_raw),
+                (w_query_hbm, w_query),
+                (w_key_hbm, w_key),
+                (w_value_hbm, w_value),
+                (ct_hbm, ct_raw),
+                (w_out_hbm, w_out),
+                (w_in_hbm, w_in),
+                (w_ffout_hbm, w_ffout),
+            )
+        )
+    ]
+    for load in loads:
+        load.start()
+    barrier = pltpu.get_barrier_semaphore()
+    for offset in range(1, 8):
+        pl.semaphore_signal(
+            barrier,
+            inc=1,
+            device_id=(row_place, lax.rem(place + offset, 8)),
+            device_id_type=MESH,
+        )
+    for offset in range(1, rows_size):
+        pl.semaphore_signal(
+            barrier,
+            inc=1,
+            device_id=(lax.rem(row_place + offset, rows_size), place),
+            device_id_type=MESH,
+        )
+
+    first_single = doc_lengths[0, 1] == 0
+    loads[0].wait()
+    x_rows[0] = jnp.where(first_single, x_raw[0], x_raw[1])
+    x_rows[1] = jnp.where(first_single, x_raw[1], x_raw[0])
+
+    def norm_row(row, _):
+        values = x_rows[row].astype(f32)
+        normed[pl.ds(pl.multiple_of(row * LANES, LANES), LANES), :] = (
+            values * inverse_rms(values) * gain_attn
+        ).astype(bf16)
+        return 0
+
+    lax.fori_loop(0, 2, norm_row, 0)
+    for load in loads[1:4]:
+        load.wait()
+
+    for part, weight in enumerate((w_query, w_key, w_value)):
+        for group in range(3):
+            made = dot_nn(normed[...], weight[:, group * 256 : (group + 1) * 256]).astype(bf16)
+            turned = made.T
+            for inside in range(4):
+                for row in range(2):
+                    qkv_send[row, group * 4 + inside, part * 64 : (part + 1) * 64, :] = turned[
+                        inside * 64 : (inside + 1) * 64, row * LANES : (row + 1) * LANES
+                    ]
+
+    pl.semaphore_wait(barrier, 7 + rows_size - 1)
+
+    def send_heads(visit):
+        def head_a(offset, inside):
+            to_chip = lax.rem(chip + offset, 4)
+            owner = to_chip * 2 + inside // 2
+            visit(0, 3 * to_chip + inside, owner, inside % 2, offset == 0)
+
+        def head_b(to_parity, inside):
+            to_chip = half * 2 + to_parity
+            owner = to_chip * 2 + min(inside, 1)
+            visit(1, 6 * to_parity + inside, owner, max(inside - 1, 0), True)
+
+        for inside in (0, 2, 1):
+            for offset in (2, 1, 3, 0):
+                head_a(offset, inside)
+            for block in ((0, 1), (2, 3), (4, 5))[(0, 2, 1).index(inside)]:
+                for to_parity in range(2):
+                    head_b(to_parity, block)
+
+    def exchange(source, to_a, to_b, send_sem, a_sem, b_sem):
+        def visit(start):
+            def go(row, head, owner, slot, maybe_mine):
+                src = source.at[row, head]
+                if row == 0:
+                    dst, sem = to_a.at[slot, place], a_sem.at[slot]
+                else:
+                    dst, sem = to_b.at[slot, lax.rem(place, 4)], b_sem.at[slot]
+
+                def remote():
+                    copy = pltpu.make_async_remote_copy(
+                        src_ref=src,
+                        dst_ref=dst,
+                        send_sem=send_sem.at[row, head],
+                        recv_sem=sem,
+                        device_id=(row_place, owner),
+                        device_id_type=MESH,
+                    )
+                    if start:
+                        copy.start()
+                    else:
+                        copy.wait_send()
+
+                if not maybe_mine:
+                    remote()
+                    return
+                pl.when(owner != place)(remote)
+                if start:
+
+                    @pl.when(owner == place)
+                    def _():
+                        pltpu.make_async_copy(src, dst, sem).start()
+
+            return go
+
+        return (lambda: send_heads(visit(True))), (lambda: send_heads(visit(False)))
+
+    start_qkv, end_qkv = exchange(qkv_send, slots_a, slots_b, qkv_send_sem, slot_a_sem, slot_b_sem)
+    start_qkv()
+
+    def back_to_sources(row, source, head, to, send_sem, sem, start):
+        count = 8 if row == 0 else 4
+        for offset in (4, 5, 3, 6, 2, 7, 1, 0) if row == 0 else (2, 3, 1, 0):
+            if row == 0:
+                index = lax.rem(place + offset, 8)
+                owner = index
+            else:
+                index = lax.rem(lax.rem(place, 4) + offset, 4)
+                owner = half * 4 + index
+            if offset:
+                copy = pltpu.make_async_remote_copy(
+                    src_ref=source.at[index],
+                    dst_ref=to.at[row, head],
+                    send_sem=send_sem.at[offset],
+                    recv_sem=sem.at[row],
+                    device_id=(row_place, owner),
+                    device_id_type=MESH,
+                )
+                if start:
+                    copy.start()
+                else:
+                    copy.wait_send()
+            elif start:
+                pltpu.make_async_copy(source.at[index], to.at[row, head], sem.at[row]).start()
+
+    head_of_a = lambda item: 3 * chip + item + 2 * core
+    head_of_b = lambda item: 6 * parity + item + core
+    count_a = 2 - core
+    count_b = 1 + 4 * core
+
+    def make_bias(slot, head):
+        offset = 256 - lax.broadcasted_iota(jnp.int32, (8, 512), 1)
+        bucket = bucket_of(offset)
+        line = jnp.zeros((8, 512), f32)
+        for number in range(32):
+            line = jnp.where(bucket == number, rel_table[head, number], line)
+        spread = pltpu.roll(
+            jnp.broadcast_to(line[:1], (128, 512)), 0, 1, stride=1, stride_axis=0
+        )
+        bias[slot, 0] = jnp.full((128, 128), rel_table[head, 15], f32)
+        bias[slot, 1] = spread[:, 384:512]
+        bias[slot, 2] = spread[:, 256:384]
+        bias[slot, 3] = spread[:, 128:256]
+        bias[slot, 4] = jnp.full((128, 128), rel_table[head, 31], f32)
+
+    def bias_a(item, _):
+        make_bias(item, head_of_a(item))
+        return 0
+
+    def bias_b(item, _):
+        make_bias(2 + item, head_of_b(item))
+        return 0
+
+    lax.fori_loop(0, count_a, bias_a, 0)
+    lax.fori_loop(0, count_b, bias_b, 0)
+
+    lane48 = lax.broadcasted_iota(jnp.int32, (4, 48), 1)
+    term = lax.broadcasted_iota(jnp.int32, (4, 48), 0)
+    fold12 = (
+        lax.rem(lax.broadcasted_iota(jnp.int32, (12, 48), 1), 12)
+        == lax.broadcasted_iota(jnp.int32, (12, 48), 0)
+    ).astype(f32)
+
+    def rule_lines(transposed, outer):
+        made = jnp.zeros((4, 48), f32)
+        for number in range(4):
+            for inner in range(4):
+                value = (
+                    phm_rule[number, inner, outer] if transposed else phm_rule[number, outer, inner]
+                )
+                made = jnp.where((term == number) & (lane48 // 12 == inner), value, made)
+        return made
+
+    down_rules = [rule_lines(False, outer) for outer in range(4)]
+    up_rules = [rule_lines(True, outer) for outer in range(4)]
+    down_right_wide = dot_nn(down_right[...], fold12, highest_p)
+    up_left_wide = dot_nn(up_left[...], fold12, highest_p)
+    down_left_t = down_left[...].T
+    up_right_t = up_right[...].T
+    for outer in range(4):
+        down_b[outer * 192 : (outer + 1) * 192, :] = dot_nn(
+            down_left_t, down_rules[outer] * down_right_wide, highest_p
+        ).astype(bf16)
+        up_b[outer * 192 : (outer + 1) * 192, :] = dot_nn(
+            up_right_t, up_rules[outer] * up_left_wide, highest_p
+        ).astype(bf16)
+
+    loads[4].wait()
+    ct_rows[0:LANES, :] = jnp.where(first_single, ct_raw[0], ct_raw[1])
+    ct_rows[LANES:, :] = jnp.where(first_single, ct_raw[1], ct_raw[0])
+
+    zero64 = jnp.zeros((64, 1024), bf16)
+
+    def turn_keys(slot, blocks):
+        for block in range(blocks):
+            key_value[block * 256 : (block + 1) * 256, :] = slot[block, 64:192, :].T
+
+    def joined(slot, tile, low, high):
+        return jnp.concatenate([slot[4 * tile + u, low:high, :] for u in range(4)], axis=1)
+
+    def with_bias(scores, number, block, tile):
+        lines = []
+        for upper in range(2):
+            pieces = []
+            for lane in range(8):
+                distance = 2 * block + upper - (8 * tile + lane)
+                if isinstance(distance, int):
+                    distance = max(-2, min(2, distance)) + 2
+                else:
+                    distance = jnp.clip(distance, -2, 2) + 2
+                pieces.append(
+                    scores[upper * 128 : (upper + 1) * 128, lane * 128 : (lane + 1) * 128]
+                    + bias[number, distance]
+                )
+            lines.append(jnp.concatenate(pieces, axis=1))
+        return jnp.concatenate(lines, axis=0)
+
+    def attend(slot, number, blocks, att, mass, o_send):
+        turn_keys(slot, blocks)
+
+        def one_tile(tile, _):
+            lanes = pl.ds(pl.multiple_of(tile * 1024, 1024), 1024)
+            query = jnp.concatenate([joined(slot, tile, 0, 64), zero64], axis=0)
+            peak = jnp.full((8, 1024), -1e30, f32)
+            for block in range(blocks):
+                scores = dot_nn(key_value[block * 256 : (block + 1) * 256, :], query)
+                scores = with_bias(scores, number, block, tile)
+                wide[block * 256 : (block + 1) * 256, :] = scores
+                peak = jnp.maximum(peak, jnp.max(scores.reshape(32, 8, 1024), axis=0))
+            peak = jnp.max(peak, axis=0, keepdims=True)
+            total = jnp.zeros((64, 1024), f32)
+            mass_sum = jnp.zeros((8, 1024), f32)
+            for block in range(blocks):
+                weights = jnp.exp(wide[block * 256 : (block + 1) * 256, :] - peak)
+                mass_sum = mass_sum + jnp.sum(weights.reshape(32, 8, 1024), axis=0)
+                total = total + dot_nn(slot[block, 128:192, :], weights.astype(bf16))
+            mass_sum = jnp.sum(mass_sum, axis=0, keepdims=True)
+            total = total / mass_sum
+            att[:, lanes] = total
+            mass[:, lanes] = peak + jnp.log(mass_sum)
+            for u in range(4):
+                o_send[4 * tile + u] = total[:, u * 256 : (u + 1) * 256].astype(bf16)
+            return 0
+
+        if blocks == 4:
+            one_tile(0, 0)
+        else:
+            lax.fori_loop(0, blocks // 4, one_tile, 0)
+
+    def forward_a(item, _):
+        pltpu.make_async_copy(slots_a.at[item], slots_a.at[item], slot_a_sem.at[item]).wait()
+        attend(slots_a.at[item], item, 8, att_a.at[item], mass_a.at[item], o_send_a.at[item])
+        back_to_sources(
+            0, o_send_a.at[item], head_of_a(item), att_recv, o_send_a_sem.at[item], att_sem, True
+        )
+        return 0
+
+    def forward_b(item, _):
+        pltpu.make_async_copy(slots_b.at[item], slots_b.at[item], slot_b_sem.at[item]).wait()
+        attend(slots_b.at[item], 2 + item, 4, att_b.at[item], mass_b.at[item], o_send_b.at[item])
+        back_to_sources(
+            1, o_send_b.at[item], head_of_b(item), att_recv, o_send_b_sem.at[item], att_sem, True
+        )
+        return 0
+
+    lax.fori_loop(0, count_a, forward_a, 0)
+    lax.fori_loop(0, count_b, forward_b, 0)
+
+    loads[5].wait()
+    for row in range(2):
+        pltpu.make_async_copy(att_recv.at[row], att_recv.at[row], att_sem.at[row]).wait()
+        lines = slice(row * LANES, (row + 1) * LANES)
+        attended = att_recv[row].reshape(768, LANES).T
+        values = x_rows[row].astype(f32) + dot_nn(attended, w_out[...])
+        hidden[lines, :] = values
+        normed[lines, :] = (values * inverse_rms(values) * gain_ffn).astype(bf16)
+
+    def wide_place(chunk):
+        return (
+            pl.ds(pl.multiple_of((chunk // 2) * 512, 512), 512),
+            pl.ds(pl.multiple_of(lax.rem(chunk, 2) * 512, 512), 512),
+        )
+
+    loads[6].wait()
+
+    def inner_chunk(chunk, _):
+        columns = pl.ds(pl.multiple_of(chunk * 512, 512), 512)
+        value, slope = gelu_pair(dot_nn(normed[...], w_in[:, columns]))
+        act[:, columns] = value.astype(bf16)
+        at_rows, at_lanes = wide_place(chunk)
+        wide[at_rows, at_lanes] = slope
+        return 0
+
+    lax.fori_loop(0, 6, inner_chunk, 0)
+    loads[7].wait()
+    ff_out[...] = dot_nn(act[...], w_ffout[...]).astype(bf16)
+    squeezed_act, squeezed_slope = gelu_pair(dot_nn(ff_out[...], down_b[...]) + down_bias)
+    squeezed_act = squeezed_act.astype(bf16)
+    squeezed_grad = dot_nn(ct_rows[...], up_b[...]) * squeezed_slope
+    squeezed_low = squeezed_grad.astype(bf16)
+    result_rows = []
+    for row in range(2):
+        lines = slice(row * LANES, (row + 1) * LANES)
+        result_rows.append(
+            (
+                hidden[lines, :]
+                + ff_out[lines, :].astype(f32)
+                + dot_nt(squeezed_act[lines, :], up_b[...])
+                + up_bias
+            ).astype(bf16)
+        )
+    out_stage[0, 0] = jnp.where(first_single, result_rows[0], result_rows[1])
+    out_stage[0, 1] = jnp.where(first_single, result_rows[1], result_rows[0])
+    write_out = pltpu.make_async_copy(out_stage.at[0], out_hbm, out_sem.at[0])
+    write_out.start()
+
+    ff_grad = (ct_rows[...].astype(f32) + dot_nt(squeezed_low, down_b[...])).astype(bf16)
+
+    normed[...] = ff_grad
+
+    def inner_back(chunk, _):
+        columns = pl.ds(pl.multiple_of(chunk * 512, 512), 512)
+        at_rows, at_lanes = wide_place(chunk)
+        act[:, columns] = (
+            dot_nt(normed[...], w_ffout[columns, :]) * wide[at_rows, at_lanes]
+        ).astype(bf16)
+        return 0
+
+    lax.fori_loop(0, 6, inner_back, 0)
+    normed_grad = dot_nt(act[...], w_in[...])
+    for row in range(2):
+        lines = slice(row * LANES, (row + 1) * LANES)
+        values = ct_rows[lines, :].astype(f32) + norm_back(
+            hidden[lines, :], gain_ffn, normed_grad[lines, :]
+        )
+        hidden_grad[lines, :] = values
+        turned = dot_nt(values.astype(bf16), w_out[...]).astype(bf16).T
+        do_send[row] = turned.reshape(12, 64, LANES)
+
+    end_qkv()
+    start_do, end_do = exchange(do_send, do_a, do_b, do_send_sem, do_a_sem, do_b_sem)
+    start_do()
+
+    up_grad = dot_nn(ct_rows[...].T, squeezed_act)
+    down_grad = dot_nn(ff_out[...].T, squeezed_low)
+    column48 = lax.broadcasted_iota(jnp.int32, (48, 16), 0) // 12
+    lane16 = lax.broadcasted_iota(jnp.int32, (48, 16), 1)
+
+    def kron_back(grad, left, right_wide, rules, transposed):
+        left_grad = jnp.zeros((4, 192), f32)
+        right_grad = jnp.zeros((4, 48), f32)
+        rule_grad = jnp.zeros((4, 16), f32)
+        for outer in range(4):
+            block = grad[outer * 192 : (outer + 1) * 192, :]
+            left_grad = left_grad + dot_nt(rules[outer] * right_wide, block, highest_p)
+            contracted = dot_nn(left, block, highest_p)
+            right_grad = right_grad + contracted * rules[outer]
+            target = column48 * 4 + outer if transposed else outer * 4 + column48
+            rule_grad = rule_grad + dot_nn(
+                contracted * right_wide, (target == lane16).astype(f32), highest_p
+            )
+        return left_grad, dot_nt(right_grad, fold12, highest_p), rule_grad
+
+    dl_grad, dr_grad, rule_down = kron_back(
+        down_grad, down_left[...], down_right_wide, down_rules, False
+    )
+    ur_grad, ul_grad, rule_up = kron_back(up_grad, up_right[...], up_left_wide, up_rules, True)
+    stats[...] = jnp.zeros_like(stats)
+    stats[0:4, 0:192] = dl_grad
+    stats[4:8, 0:192] = ur_grad
+    stats[8:12, 0:12] = dr_grad
+    stats[8:12, 128:140] = ul_grad
+    stats[12:16, 0:16] = rule_down + rule_up
+    stats[16:17, 0:48] = jnp.sum(squeezed_grad, axis=0, keepdims=True)
+    up_bias_grad = jnp.sum(ct_rows[...].astype(f32), axis=0, keepdims=True)
+    for third in range(3):
+        stats[17 + third : 18 + third, :] = up_bias_grad[:, third * 256 : (third + 1) * 256]
+
+    def rows_copy(offset):
+        return pltpu.make_async_remote_copy(
+            src_ref=stats,
+            dst_ref=stats_rows.at[row_place],
+            send_sem=st_rows_send.at[offset - 1],
+            recv_sem=st_rows_recv.at[offset - 1],
+            device_id=(lax.rem(row_place + offset, rows_size), place),
+            device_id_type=MESH,
+        )
+
+    for offset in range(1, rows_size):
+        rows_copy(offset).start()
+
+    def attend_back(slot, do_slot, number, blocks, att, mass, g_send):
+        turn_keys(slot, blocks)
+
+        def one_tile(tile, first):
+            lanes = pl.ds(pl.multiple_of(tile * 1024, 1024), 1024)
+            query = joined(slot, tile, 0, 64)
+            grad = joined(do_slot, tile, 0, 64)
+            query_z = jnp.concatenate([query, zero64], axis=0)
+            grad_z = jnp.concatenate([zero64, grad], axis=0)
+            delta = jnp.sum(grad.astype(f32) * att[:, lanes], axis=0, keepdims=True)
+            log_mass = mass[:, lanes]
+            for block in range(blocks):
+                keys = slice(block * 256, (block + 1) * 256)
+                scores = with_bias(dot_nn(key_value[keys, :], query_z), number, block, tile)
+                probs = jnp.exp(scores - log_mass)
+                probs_grad = dot_nn(key_value[keys, :], grad_z)
+                score_grad = (probs * (probs_grad - delta)).astype(bf16)
+                dq_part = dot_nn(slot[block, 64:128, :], score_grad)
+                if block == 0:
+                    dq_acc[...] = dq_part
+                else:
+                    dq_acc[...] += dq_part
+                dv_part = dot_nt(grad, probs.astype(bf16))
+                dk_part = dot_nt(query, score_grad)
+                if first:
+                    dv_acc[:, keys] = dv_part
+                    dk_acc[:, keys] = dk_part
+                else:
+                    dv_acc[:, keys] += dv_part
+                    dk_acc[:, keys] += dk_part
+            for u in range(4):
+                g_send[4 * tile + u, 0:64, :] = dq_acc[:, u * 256 : (u + 1) * 256].astype(bf16)
+
+        for tile in range(blocks // 4):
+            one_tile(tile, tile == 0)
+        for block in range(blocks):
+            keys = slice(block * 256, (block + 1) * 256)
+            g_send[block, 64:128, :] = dk_acc[:, keys].astype(bf16)
+            g_send[block, 128:192, :] = dv_acc[:, keys].astype(bf16)
+
+    def backward_a(item, _):
+        pltpu.make_async_copy(do_a.at[item], do_a.at[item], do_a_sem.at[item]).wait()
+        attend_back(
+            slots_a.at[item],
+            do_a.at[item],
+            item,
+            8,
+            att_a.at[item],
+            mass_a.at[item],
+            slots_a.at[item],
+        )
+        back_to_sources(
+            0, slots_a.at[item], head_of_a(item), g_recv, g_send_a_sem.at[item], g_sem, True
+        )
+        return 0
+
+    def backward_b(item, _):
+        pltpu.make_async_copy(do_b.at[item], do_b.at[item], do_b_sem.at[item]).wait()
+        attend_back(
+            slots_b.at[item],
+            do_b.at[item],
+            2 + item,
+            4,
+            att_b.at[item],
+            mass_b.at[item],
+            slots_b.at[item],
+        )
+        back_to_sources(
+            1, slots_b.at[item], head_of_b(item), g_recv, g_send_b_sem.at[item], g_sem, True
+        )
+        return 0
+
+    lax.fori_loop(0, count_a, backward_a, 0)
+
+    my_lanes = pl.ds(pl.multiple_of(core * 128, 128), 128)
+    other_lanes = pl.ds(pl.multiple_of((1 - core) * 128, 128), 128)
+    sibling = chip * 2 + 1 - core
+    stats_rows[row_place] = stats[...]
+    for offset in range(1, rows_size):
+        rows_copy(offset).wait()
+    summed = stats_rows[0]
+    for number in range(1, rows_size):
+        summed = summed + stats_rows[number]
+    stats_core[0] = summed
+    core_copy = pltpu.make_async_remote_copy(
+        src_ref=stats_core.at[0, :, other_lanes],
+        dst_ref=stats_core.at[1, :, other_lanes],
+        send_sem=st_core_send,
+        recv_sem=st_core_recv,
+        device_id=(row_place, sibling),
+        device_id_type=MESH,
+    )
+    core_copy.start()
+    core_copy.wait_send()
+    pltpu.make_async_copy(
+        stats_core.at[1, :, my_lanes], stats_core.at[1, :, my_lanes], st_core_recv
+    ).wait()
+    stats_z[chip] = stats_core[0, :, my_lanes] + stats_core[1, :, my_lanes]
+
+    def z_copy(offset):
+        return pltpu.make_async_remote_copy(
+            src_ref=stats_z.at[chip],
+            dst_ref=stats_z.at[chip],
+            send_sem=st_z_send.at[offset - 1],
+            recv_sem=st_z_recv.at[offset - 1],
+            device_id=(row_place, lax.rem(chip + offset, 4) * 2 + core),
+            device_id_type=MESH,
+        )
+
+    for offset in range(1, 4):
+        z_copy(offset).start()
+
+    lax.fori_loop(0, count_b, backward_b, 0)
+
+    for offset in range(1, 4):
+        z_copy(offset).wait()
+    stats_core[2, :, my_lanes] = (stats_z[0] + stats_z[1]) + (stats_z[2] + stats_z[3])
+    last_copy = pltpu.make_async_remote_copy(
+        src_ref=stats_core.at[2, :, my_lanes],
+        dst_ref=stats_core.at[2, :, my_lanes],
+        send_sem=st_last_send,
+        recv_sem=st_last_recv,
+        device_id=(row_place, sibling),
+        device_id_type=MESH,
+    )
+    last_copy.start()
+
+    turned_grad = jnp.zeros((768, 512), f32)
+    for row in range(2):
+        pltpu.make_async_copy(g_recv.at[row], g_recv.at[row], g_sem.at[row]).wait()
+    for part, weight in enumerate((w_query, w_key, w_value)):
+        grads = jnp.concatenate(
+            [
+                g_recv[row, :, part * 64 : (part + 1) * 64, :].reshape(768, LANES)
+                for row in range(2)
+            ],
+            axis=1,
+        )
+        turned_grad = turned_grad + dot_nn(weight[...], grads)
+    final_rows = []
+    for row in range(2):
+        lines = slice(row * LANES, (row + 1) * LANES)
+        final_rows.append(
+            (
+                hidden_grad[lines, :]
+                + norm_back(
+                    x_rows[row].astype(f32), gain_attn, turned_grad[:, lines].T
+                )
+            ).astype(bf16)
+        )
+    out_stage[1, 0] = jnp.where(first_single, final_rows[0], final_rows[1])
+    out_stage[1, 1] = jnp.where(first_single, final_rows[1], final_rows[0])
+    write_grad = pltpu.make_async_copy(out_stage.at[1], igrad_hbm, out_sem.at[1])
+    write_grad.start()
+
+    last_copy.wait_send()
+    pltpu.make_async_copy(
+        stats_core.at[2, :, other_lanes], stats_core.at[2, :, other_lanes], st_last_recv
+    ).wait()
+    stats_out[...] = stats_core[2]
+
+    end_do()
+
+    def end_a(item, _):
+        head = head_of_a(item)
+        back_to_sources(
+            0, o_send_a.at[item], head, att_recv, o_send_a_sem.at[item], att_sem, False
+        )
+        back_to_sources(0, slots_a.at[item], head, g_recv, g_send_a_sem.at[item], g_sem, False)
+        return 0
+
+    def end_b(item, _):
+        head = head_of_b(item)
+        back_to_sources(
+            1, o_send_b.at[item], head, att_recv, o_send_b_sem.at[item], att_sem, False
+        )
+        back_to_sources(1, slots_b.at[item], head, g_recv, g_send_b_sem.at[item], g_sem, False)
+        return 0
+
+    lax.fori_loop(0, count_a, end_a, 0)
+    lax.fori_loop(0, count_b, end_b, 0)
+    write_out.wait()
+    write_grad.wait()
+
+
+def finish_kernel(
+    stats,
+    out_from,
+    grad_from,
+    out_to,
+    grad_to,
+    rule_out,
+    dl_out,
+    dr_out,
+    ul_out,
+    ur_out,
+    db_out,
+    ub_out,
+    stage,
+    sem,
+):
+    gets, puts = [], []
+    for number, (source, target) in enumerate(((grad_from, grad_to), (out_from, out_to))):
+        for row in range(2):
+            gets.append(
+                pltpu.make_async_copy(
+                    source.at[row], stage.at[number, row], sem.at[0, number, row]
+                )
+            )
+            puts.append(
+                pltpu.make_async_copy(
+                    stage.at[number, row], target.at[row], sem.at[1, number, row]
+                )
+            )
+    for get in gets:
+        get.start()
+    for outer in range(4):
+        rule_out[:, outer, :] = stats[12:16, 4 * outer : 4 * outer + 4]
+    dl_out[...] = stats[0:4, 0:192]
+    ur_out[...] = stats[4:8, 0:192]
+    dr_out[...] = stats[8:12, 0:12]
+    ul_out[...] = stats[8:12, 128:140]
+    db_out[...] = stats[16:17, 0:48].reshape(48)
+    ub_out[...] = jnp.concatenate([stats[17 + third : 18 + third, :] for third in range(3)], axis=1).reshape(768)
+    for get, put in zip(gets, puts):
+        get.wait()
+        put.start()
+    for put in puts:
+        put.wait()
+
+
+def layer_on_slice(rows_size, *arrays):
+    (
+        inputs,
+        doc_lengths,
+        w_query,
+        w_key,
+        w_value,
+        w_out,
+        w_in,
+        w_ffout,
+        rel_table,
+        gain_attn,
+        gain_ffn,
+        phm_rule,
+        down_left,
+        down_right,
+        up_left,
+        up_right,
+        down_bias,
+        up_bias,
+        cotangent,
+    ) = arrays
+    f32 = jnp.float32
+    bf16 = jnp.bfloat16
+    shape = jax.ShapeDtypeStruct
+    vmem = pl.BlockSpec(memory_space=pltpu.VMEM)
+    smem = pl.BlockSpec(memory_space=pltpu.SMEM)
+    hbm = pl.BlockSpec(memory_space=pl.ANY)
+    dma = pltpu.SemaphoreType.DMA
+    results = pl.pallas_call(
+        functools.partial(layer_kernel, rows_size),
+        out_shape=[
+            shape(inputs.shape, bf16),
+            shape(inputs.shape, bf16),
+            shape((24, 256), f32),
+        ],
+        in_specs=[smem] * 3 + [vmem] * 8 + [hbm] * 8,
+        out_specs=[hbm] * 2 + [vmem],
+        scratch_shapes=[
+            pltpu.VMEM((768, 768), bf16),
+            pltpu.VMEM((768, 768), bf16),
+            pltpu.VMEM((768, 768), bf16),
+            pltpu.VMEM((768, 768), bf16),
+            pltpu.VMEM((768, 3072), bf16),
+            pltpu.VMEM((3072, 768), bf16),
+            pltpu.VMEM((2, LANES, 768), bf16),
+            pltpu.VMEM((512, 768), bf16),
+            pltpu.VMEM((512, 768), bf16),
+            pltpu.VMEM((2, 12, 192, LANES), bf16),
+            pltpu.VMEM((2, 8, 192, LANES), bf16),
+            pltpu.VMEM((5, 4, 192, LANES), bf16),
+            pltpu.VMEM((2048, 128), bf16),
+            pltpu.VMEM((2048, 1024), f32),
+            pltpu.VMEM((7, 5, 128, 128), f32),
+            pltpu.VMEM((2, 64, 2048), f32),
+            pltpu.VMEM((5, 64, 1024), f32),
+            pltpu.VMEM((2, 1, 2048), f32),
+            pltpu.VMEM((5, 1, 1024), f32),
+            pltpu.VMEM((2, 8, 64, LANES), bf16),
+            pltpu.VMEM((5, 4, 64, LANES), bf16),
+            pltpu.VMEM((2, 12, 64, LANES), bf16),
+            pltpu.VMEM((512, 768), f32),
+            pltpu.VMEM((512, 3072), bf16),
+            pltpu.VMEM((512, 768), bf16),
+            pltpu.VMEM((768, 48), bf16),
+            pltpu.VMEM((768, 48), bf16),
+            pltpu.VMEM((512, 768), f32),
+            pltpu.VMEM((2, 8, 64, LANES), bf16),
+            pltpu.VMEM((5, 4, 64, LANES), bf16),
+            pltpu.VMEM((64, 2048), f32),
+            pltpu.VMEM((64, 2048), f32),
+            pltpu.VMEM((64, 1024), f32),
+            pltpu.VMEM((24, 256), f32),
+            pltpu.VMEM((rows_size, 24, 256), f32),
+            pltpu.VMEM((3, 24, 256), f32),
+            pltpu.VMEM((4, 24, 128), f32),
+            pltpu.VMEM((2, 2, LANES, 768), bf16),
+            dma((8,)),
+            dma((2, 12)),
+            dma((2,)),
+            dma((5,)),
+            dma((2, 8)),
+            dma((5, 4)),
+            dma((2,)),
+            dma((2, 12)),
+            dma((2,)),
+            dma((5,)),
+            dma((2, 8)),
+            dma((5, 4)),
+            dma((2,)),
+            dma((max(rows_size - 1, 1),)),
+            dma((max(rows_size - 1, 1),)),
+            dma(()),
+            dma(()),
+            dma((3,)),
+            dma((3,)),
+            dma(()),
+            dma(()),
+            dma((2,)),
+        ],
+        compiler_params=pltpu.CompilerParams(
+            collective_id=0, has_side_effects=True, vmem_limit_bytes=56 * 1024 * 1024
+        ),
+        name="encoder_layer",
+    )(
+        doc_lengths,
+        rel_table.T,
+        phm_rule,
+        gain_attn,
+        gain_ffn,
+        down_left,
+        down_right,
+        up_left,
+        up_right,
+        down_bias,
+        up_bias,
+        inputs,
+        cotangent,
+        w_query,
+        w_key,
+        w_value,
+        w_out,
+        w_in,
+        w_ffout,
+    )
+    return pl.pallas_call(
+        finish_kernel,
+        out_shape=[
+            shape(inputs.shape, bf16),
+            shape(inputs.shape, bf16),
+            shape(phm_rule.shape, f32),
+            shape((4, 192), f32),
+            shape((4, 12), f32),
+            shape((4, 12), f32),
+            shape((4, 192), f32),
+            shape((48,), f32),
+            shape((768,), f32),
+        ],
+        in_specs=[vmem] + [hbm] * 2,
+        out_specs=[hbm] * 2 + [vmem] * 7,
+        scratch_shapes=[pltpu.VMEM((2, 2, LANES, 768), bf16), dma((2, 2, 2))],
+        name="finish",
+    )(results[2], results[0], results[1])
+
+
+def pick(rows_size, seq_size, *arrays):
+    inputs, doc_lengths = arrays[:2]
+    fits = (
+        seq_size == 8
+        and inputs.shape == (2, LANES, 768)
+        and doc_lengths.shape == (2, 2)
+        and arrays[8].shape == (32, 12)
+        and arrays[6].shape == (768, 3072)
+    )
+    return layer_on_slice(rows_size, *arrays) if fits else local(*arrays)
+
+
 def solution(mesh):
     return jax.shard_map(
-        local,
+        functools.partial(pick, mesh.shape["rows"], mesh.shape["seq"]),
         mesh=mesh,
         in_specs=(
             P("rows", "seq", None),

time: 896 us -> 138 us (0.15); the launches traced: 886 us -> 138 us
  matrix products: 427 us -> 0 us
  local copies, waits for them, and re-layouts: 182 us -> 0 us
  Pallas kernels: 0 us -> 137 us
  waiting for transfers between devices: 105 us -> 0 us
  other arithmetic: 72.9 us -> 0 us
  blocking collectives: 69.2 us -> 0 us
  loops' own time: 14.8 us -> 0 us
  between operations: 15.1 us -> 0.86 us
    dot_general x79 -> x0, matrix products: 427 us -> none  [the longest x12 79.6 us: pair_bias(): jnp.einsum('qkb,bh->qhk', onehot, table_high, preferred_element_type=jnp....]
    pallas_call x0 -> x2, Pallas kernels: none -> 137 us  [the longest x1 133 us: layer_on_slice(): pl.pallas_call(functools.partial(layer_kernel, rows_size), out_shape=[sha...]
    all_gather x4 -> x0, waiting for transfers between devices: 105 us -> none  [the longest x1 65 us: local(): lax.all_gather(value_rows, 'seq', axis=1, tiled=True)]
    add x12 -> x0, local copies, waits for them, and re-layouts: 99 us -> none  [pair_bias(): return high_part + rest_part]
    reduce_sum x20 -> x0, other arithmetic: 48.8 us -> none  [the longest x4 35.1 us: forward_piece(): mass_sum = mass_sum * rescale + jnp.sum(weights, axis=-1)]
    psum x1 -> x0, blocking collectives: 39.6 us -> none  [local(): lax.psum((rule_down + rule_up, down_left_grad, down_right_grad, up_left_g...]
    dynamic_slice x24 -> x0, local copies, waits for them, and re-layouts: 38 us -> none  [the longest x12 31.4 us: one_step(): lax.dynamic_slice_in_dim(member, begin_row, block_len, 1)]
    all_gather x2 -> x0, blocking collectives: 29.6 us -> none  [the longest x1 15.3 us: local(): lax.all_gather(log_mass, 'seq', axis=1, tiled=True)]
  transfers between devices with their start and end apart: 4 -> 0, of which waited for: 2 -> 0; matrix products, arithmetic and copies ran while one was open for 50% -> 0% of each run, Pallas kernels for 0% -> 0%
where the time goes in v1:
time: 138 us
  Pallas kernels  137 us (99%)
    pallas_call x1, Pallas kernels, layer_on_slice(): pl.pallas_call(functools.partial(layer_kernel, rows_size), out_shape=[sha...  133 us
    pallas_call x1, Pallas kernels, layer_on_slice(): pl.pallas_call(finish_kernel, out_shape=[shape(inputs.shape, bf16), shape...  3.56 us

profile of v1, /device:TPU:0, one launch (start us, length us, event | category | flops | bytes accessed | tf_op | source)
XLA Modules:
  0.0 137.9 jit_solution(10260311506882677375)
XLA Ops:
  0.7 133.5 %encoder_layer.1 = (bf16[2,256,768]{2,1,0:T(8,128)(2,1)}, bf16[2,256,768]{2,1,0:T(8,128)(2,1)}, f32[24,256]{1,0:T(8,128)}) custom-call(s32[2,2]{1,0:T(2,128)} %doc_lengths.1, f32[12,32]{1,0:T(8,128)} %bitcast.1, f32[4,4,4]{2,1,0:T(4,128)} %phm_rule.1, f32[768]{0:T(1024)} %gain_attn.1, f32[768]{0:T(1024)} %gain_ffn.1, f32[4,192]{1,0:T(4,128)} %down_left.1, ...), custom_call_target="tpu_custom_call" | custom-call | tf_op jit(solution)/shard_map/encoder_layer/pallas_call | solution.py:1174
  134.1 3.6 %finish.1 = (bf16[2,256,768]{2,1,0:T(8,128)(2,1)}, bf16[2,256,768]{2,1,0:T(8,128)(2,1)}, f32[4,4,4]{2,1,0:T(4,128)}, f32[4,192]{1,0:T(4,128)}, f32[4,12]{1,0:T(4...) custom-call(f32[24,256]{1,0:T(8,128)} %get-tuple-element.12.stats, ...), custom_call_target="tpu_custom_call" | custom-call | tf_op jit(solution)/shard_map/finish/pallas_call | solution.py:1270
